TPU v7x, 32 devices: a whole 2x2x4 slice. The times are simulated.
32 devices in a mesh: kloop: 16 (over z, y, x), pair: 2 (over core).
Axes of the slice: x: 2, y: 2, z: 4, core: 2. Of those that a mesh axis runs over, the one named last changes fastest.
Arguments:
- orbitals: bfloat16 [32, 32, 512], P('kloop'), may hold values from -6 to 6
- fitting: bfloat16 [512, 1400], replicated, may hold values from -0.25 to 0.25
- screen: bfloat16 [4, 1400, 1400], P(None, None, 'pair'), may hold values from -0.00390625 to 0.00390625
- coulomb: float32 [1400], replicated, may hold values from 0.005 to 0.1
- qindex: int32 [32, 2], replicated, may hold values from 0 to 3
Outputs:
- kernel: bfloat16 [32, 2, 256, 256], P('kloop', None, 'pair')
Inputs may be any that keep to these rules, and one draw needn't show every extreme that they name: `qindex`: the index of the held screened interaction for each block.
All inputs are finite; a program needn't handle non-finite values.
Results may differ from a plain program's by a relative error of at most 0.0085.
Values may be sent and summed in bfloat16 or wider, within the bound.
A program may use at most 64 MiB of HBM per device.

v0:
```python
import jax
import jax.numpy as jnp
from jax import lax
from jax.sharding import PartitionSpec as P

NV = 16
NC = 16
S = 2


def from_behind(value, axis, steps):
    count = lax.axis_size(axis)
    pairs = [(source, (source + steps) % count) for source in range(count)]
    return lax.ppermute(value, axis, pairs)


def pair_fields(left_bands, right_bands, fitting):
    products = (
        left_bands.astype(jnp.float32)[:, None, :] * right_bands.astype(jnp.float32)[None, :, :]
    ).astype(jnp.bfloat16)
    flat = products.reshape(left_bands.shape[0] * right_bands.shape[0], left_bands.shape[1])
    return jnp.dot(flat, fitting, preferred_element_type=jnp.float32).astype(jnp.bfloat16)


def shards(orbitals, fitting, screen, coulomb, qindex):
    per_dev = orbitals.shape[0]
    pair_count = lax.axis_size("pair")
    pair_index = lax.axis_index("pair")
    loop_count = lax.axis_size("kloop")
    loop_index = lax.axis_index("kloop")
    kpoints_all = per_dev * loop_count
    slice_width = screen.shape[2]
    val_rows = NV // pair_count
    fitting_part = lax.dynamic_slice_in_dim(fitting, pair_index * slice_width, slice_width, 1)

    def row_weighted(orbital):
        chosen = lax.dynamic_slice_in_dim(orbital[:NV], pair_index * val_rows, val_rows, 0)
        fields = pair_fields(chosen, orbital[NV:], fitting)
        return (fields.astype(jnp.float32) * coulomb).astype(jnp.bfloat16)

    stacked = []
    own_weighted = [row_weighted(orbitals[local_k]) for local_k in range(per_dev)]
    for shift_step in range(1, S + 1):
        arrived = from_behind(orbitals, "kloop", shift_step)
        blocks = []
        for local_k in range(per_dev):
            column = ((loop_index - shift_step) * per_dev + local_k) % kpoints_all
            column_orbital = arrived[local_k]
            row_orb = orbitals[local_k]
            col_orb = arrived[local_k]
            q_pick = qindex[column, shift_step - 1]
            interaction = lax.dynamic_index_in_dim(screen, q_pick, 0, keepdims=False)
            vale = pair_fields(row_orb[:NV], col_orb[:NV], fitting_part).reshape(
                NV, NV, slice_width
            )
            cond = pair_fields(row_orb[NV:], col_orb[NV:], fitting)
            screened = jnp.dot(cond, interaction, preferred_element_type=jnp.float32)
            screened = screened.astype(jnp.bfloat16).reshape(NC, NC, slice_width)
            terms = jnp.einsum("xyg,vwg->vxwy", screened, vale, preferred_element_type=jnp.float32)
            direct = lax.psum_scatter(
                terms.reshape(val_rows * NC * lax.axis_size("pair"), NV * NC).astype(jnp.bfloat16),
                "pair",
                scatter_dimension=0,
                tiled=True,
            ).astype(jnp.float32)
            exchange = lax.dot_general(
                own_weighted[local_k],
                pair_fields(column_orbital[:NV], column_orbital[NV:], fitting),
                (((1,), (1,)), ((), ())),
                preferred_element_type=jnp.float32,
            )
            blocks.append((2.0 * exchange - direct).astype(jnp.bfloat16))
        computed = jnp.stack(blocks, 0)
        stacked.append(from_behind(computed, "kloop", -shift_step))
    return jnp.stack(stacked, axis=1)


def solution(mesh):
    return jax.shard_map(
        shards,
        mesh=mesh,
        in_specs=(P("kloop", None, None), P(), P(None, None, "pair"), P(), P()),
        out_specs=P("kloop", None, "pair", None),
        check_vma=False,
    )
```

profile of v0, /device:TPU:0, one launch (start us, length us, event | category | flops | bytes accessed | tf_op | source)
XLA Modules:
  0.0 123.4 jit_solution(11067886341151988544)
XLA Ops:
  6.5 2.9 %collective-permute-start = (bf16[2,32,512]{2,1,0:T(8,128)(2,1)}, bf16[2,32,512]{2,1,0:T(8,128)(2,1)S(1)}, u32[]{:S(2)}, u32[]{:S(2)}) collective-permute-start(bf16[2,32,512]{2,1,0:T(8,128)(2,1)} %param.5), channel_id=1, source_target_pairs={{0,2},{2,4},{4,6},{6,8},{8,10},{10,12},{12,14},{14,16},{16,18},{18... | collective-permute-start | bytes 196616 | tf_op jit(solution)/shard_map/ppermute | solution.py:14
  9.5 1.5 %collective-permute-start.2 = (bf16[2,32,512]{2,1,0:T(8,128)(2,1)}, bf16[2,32,512]{2,1,0:T(8,128)(2,1)S(1)}, u32[]{:S(2)}, u32[]{:S(2)}) collective-permute-start(bf16[2,32,512]{2,1,0:T(8,128)(2,1)} %param.5), channel_id=1, source_target_pairs={{0,4},{2,6},{4,8},{6,10},{8,12},{10,14},{12,16},{14,18},{16,20},{1... | collective-permute-start | bytes 196616 | tf_op jit(solution)/shard_map/ppermute | solution.py:14
  11.0 1.5 %constant_dynamic-slice_fusion.5 = (s32[1,1]{0,1:T(1,128)}, s32[1,1]{0,1:T(1,128)}, s32[1,1]{0,1:T(1,128)}, s32[1,1]{0,1:T(1,128)}) fusion(s32[32,2]{0,1:T(2,128)} %param.9, s32[]{:T(128)S(6)} %select_n.54, s32[]{:T(128)S(6)} %select_n.57, s32[]{:T(128)S(6)} %select_n.63, s32[]{:T(128)S(6)} %select_n.60), kind=kLoop, calls=%fused_computation.111 | loop fusion | bytes 48 | tf_op jit(solution)/shard_map/dynamic_slice | solution.py:51
  17.5 0.8 bitcast_convert_fusion.1
  20.9 2.0 %fusion.5 = bf16[128,1400]{0,1:T(8,128)(2,1)} fusion(bf16[128,512]{1,0:T(8,128)(2,1)S(1)} %bitcast.195, bf16[512,1400]{0,1:T(8,128)(2,1)S(1)} %copy-done, f32[1400]{0:T(1024)} %param.8), kind=kOutput, calls=%fused_computation.15 | convolution fusion | flops 184217600 | bytes 1928672 | tf_op jit(solution)/shard_map/dot_general | solution.py:22
  22.9 25.8 %constant_dynamic-slice_fusion.4 = (bf16[1,1400,700]{1,0,2:T(2,128)(2,1)}, bf16[1,1400,700]{1,0,2:T(2,128)(2,1)}, bf16[1,1400,700]{1,0,2:T(2,128)(2,1)}, bf16[1,1400,700]{1,0,2:T(2,128)(2,1)}) fusion(bf16[4,1400,700]{1,0,2:T(4,128)(2,1)} %param.7, s32[]{:T(128)S(6)} %select_n.55, s32[]{:T(128)S(6)} %select_n.61, s32[]{:T(128)S(6)} %select_n.58, s32[]{:T(128)S(6)} %select_n.64), kind=kLoop, calls=%fused_computation.110 | loop fusion | bytes 15680016 | tf_op jit(solution)/shard_map/jit(dynamic_index_in_dim)/dynamic_slice | solution.py:52
  48.7 1.3 %fusion.2 = bf16[128,1400]{0,1:T(8,128)(2,1)} fusion(bf16[128,512]{1,0:T(8,128)(2,1)S(1)} %bitcast.194, bf16[512,1400]{0,1:T(8,128)(2,1)S(1)} %copy-done, f32[1400]{0:T(1024)S(1)} %copy-done.9), kind=kOutput, calls=%fused_computation.11 | convolution fusion | flops 184217600 | bytes 1928672 | tf_op jit(solution)/shard_map/dot_general | solution.py:22
  50.1 1.7 %multiply_convert_fusion.6 = (bf16[16,16,512]{2,1,0:T(8,128)(2,1)}, bf16[16,16,512]{2,1,0:T(8,128)(2,1)}, bf16[16,16,512]{2,1,0:T(8,128)(2,1)S(1)}, bf16[16,16,5...) fusion(f32[16,512]{1,0:T(8,128)S(1)} %get-tuple-element.18, ...), kind=kLoop, calls=%fused_computation.66 | loop fusion | flops 3145728 | bytes 3538944 | tf_op jit(solution)/shard_map/convert_element_type | solution.py:20
  51.8 3.3 %fusion.18 = bf16[256,700]{0,1:T(8,128)(2,1)S(1)} fusion(bf16[1,1400,700]{1,0,2:T(2,128)(2,1)} %get-tuple-element.5, bf16[256,512]{1,0:T(8,128)(2,1)S(1)} %bitcast.211, bf16[512,1400]{0,1:T(8,128)(2,1)S(1)} %copy-done), kind=kOutput, calls=%fused_computation.36 | convolution fusion | flops 869299200 | bytes 4014144 | tf_op jit(solution)/shard_map/dot_general | solution.py:57
  55.1 0.2 copy.17
  55.3 0.4 convolution_convert_fusion.17
  55.7 0.9 copy.15
  56.6 3.0 %fusion.10 = bf16[16,16,16,16]{3,2,1,0:T(8,128)(2,1)} fusion(bf16[16,16,700,1]{2,1,3,0:T(8,128)(2,1)} %bitcast.203, bf16[16,16,700,1]{2,1,0,3:T(8,128)(2,1)S(1)} %bitcast.201), kind=kOutput, calls=%fused_computation.28 | convolution fusion | flops 91815936 | bytes 847872 | tf_op jit(solution)/shard_map/xyg,vwg->vxwy/dot_general | solution.py:59
  59.7 2.8 %convert_element_type.367 = bf16[256,256]{1,0:T(8,128)(2,1)} reshape(bf16[16,16,16,16]{3,2,1,0:T(8,128)(2,1)} %fusion.10) | data formatting | bytes 262144 | tf_op jit(solution)/shard_map/convert_element_type | solution.py:61
  62.5 0.2 reduce-scatter.7.cloned.1.call-start
  62.8 3.3 %fusion.19 = bf16[256,700]{0,1:T(8,128)(2,1)S(1)} fusion(bf16[1,1400,700]{1,0,2:T(2,128)(2,1)} %get-tuple-element.7, bf16[256,512]{1,0:T(8,128)(2,1)S(1)} %bitcast.210, bf16[512,1400]{0,1:T(8,128)(2,1)S(1)} %copy-done), kind=kOutput, calls=%fused_computation.37 | convolution fusion | flops 869299200 | bytes 4014144 | tf_op jit(solution)/shard_map/dot_general | solution.py:57
  66.0 0.9 copy.20
  67.0 0.4 convolution_convert_fusion.16
  67.4 1.0 copy.18
  68.4 3.3 %fusion.20 = bf16[256,700]{0,1:T(8,128)(2,1)S(1)} fusion(bf16[1,1400,700]{1,0,2:T(2,128)(2,1)} %get-tuple-element.6, bf16[256,512]{1,0:T(8,128)(2,1)S(1)} %bitcast.209, bf16[512,1400]{0,1:T(8,128)(2,1)S(1)} %copy-done), kind=kOutput, calls=%fused_computation.38 | convolution fusion | flops 869299200 | bytes 4014144 | tf_op jit(solution)/shard_map/dot_general | solution.py:57
  71.7 2.1 %fusion.11 = bf16[16,16,16,16]{3,2,1,0:T(8,128)(2,1)S(1)} fusion(bf16[16,16,700,1]{2,1,3,0:T(8,128)(2,1)} %bitcast.202, bf16[16,16,700,1]{2,1,0,3:T(8,128)(2,1)} %bitcast.200), kind=kOutput, calls=%fused_computation.29 | convolution fusion | flops 91815936 | bytes 847872 | tf_op jit(solution)/shard_map/xyg,vwg->vxwy/dot_general | solution.py:59
  73.8 1.7 %convert_element_type.393 = bf16[256,256]{1,0:T(8,128)(2,1)} reshape(bf16[16,16,16,16]{3,2,1,0:T(8,128)(2,1)S(1)} %fusion.11) | data formatting | bytes 262144 | tf_op jit(solution)/shard_map/convert_element_type | solution.py:61
  75.4 0.2 copy.23
  75.6 0.4 convolution_convert_fusion.15
  76.0 0.9 copy.21
  77.0 0.0 reduce-scatter.9.cloned.1.call-start
  77.0 3.3 %fusion.21 = bf16[256,700]{0,1:T(8,128)(2,1)S(1)} fusion(bf16[1,1400,700]{1,0,2:T(2,128)(2,1)} %get-tuple-element.8, bf16[256,512]{1,0:T(8,128)(2,1)S(1)} %bitcast.208, bf16[512,1400]{0,1:T(8,128)(2,1)S(1)} %copy-done), kind=kOutput, calls=%fused_computation.39 | convolution fusion | flops 869299200 | bytes 4014144 | tf_op jit(solution)/shard_map/dot_general | solution.py:57
  80.3 2.0 %fusion.12 = bf16[16,16,16,16]{3,2,1,0:T(8,128)(2,1)S(1)} fusion(bf16[16,16,700,1]{2,1,3,0:T(8,128)(2,1)} %bitcast.197, bf16[16,16,700,1]{2,1,0,3:T(8,128)(2,1)S(1)} %bitcast.196), kind=kOutput, calls=%fused_computation.30 | convolution fusion | flops 91815936 | bytes 847872 | tf_op jit(solution)/shard_map/xyg,vwg->vxwy/dot_general | solution.py:59
  82.3 1.6 %convert_element_type.410 = bf16[256,256]{1,0:T(8,128)(2,1)} reshape(bf16[16,16,16,16]{3,2,1,0:T(8,128)(2,1)S(1)} %fusion.12) | data formatting | bytes 262144 | tf_op jit(solution)/shard_map/convert_element_type | solution.py:61
  84.0 0.2 copy.26
  84.1 0.4 convolution_convert_fusion.14
  84.5 0.2 copy.24
  84.7 0.0 reduce-scatter.9.cloned.1.call-update
  84.7 0.0 reduce-scatter.11.cloned.1.call-start
  84.8 1.0 fusion.13
  85.8 1.7 %convert_element_type.427 = bf16[256,256]{1,0:T(8,128)(2,1)} reshape(bf16[16,16,16,16]{3,2,1,0:T(8,128)(2,1)S(1)} %fusion.13) | data formatting | bytes 262144 | tf_op jit(solution)/shard_map/convert_element_type | solution.py:61
  87.5 0.0 reduce-scatter.5.cloned.1.call-done
  87.5 1.9 %fusion.34 = bf16[1,128,256]{2,1,0:T(8,128)(2,1)S(1)} fusion(bf16[128,1400]{0,1:T(8,128)(2,1)} %fusion.5, bf16[256,512]{1,0:T(8,128)(2,1)S(1)} %bitcast.207, bf16[512,1400]{0,1:T(8,128)(2,1)S(1)} %copy-done, bf16[128,256]{1,0:T(8,128)(2,1)} %reduce-scatter.5.cloned.1.call-done), kind=kOutput, calls=%fused_computation.56 | convolution fusion | flops 459241472 | bytes 2185216 | tf_op jit(solution)/shard_map/dot_general | solution.py:66
  89.5 0.0 reduce-scatter.7.cloned.1.call-done
  89.5 1.8 %fusion.35 = bf16[1,128,256]{2,1,0:T(8,128)(2,1)S(1)} fusion(bf16[128,1400]{0,1:T(8,128)(2,1)S(1)} %copy-done.2, bf16[256,512]{1,0:T(8,128)(2,1)S(1)} %bitcast.206, bf16[512,1400]{0,1:T(8,128)(2,1)S(1)} %copy-done, bf16[128,256]{1,0:T(8,128)(2,1)} %reduce-scatter.7.cloned.1.call-done), kind=kOutput, calls=%fused_computation.57 | convolution fusion | flops 459241472 | bytes 2185216 | tf_op jit(solution)/shard_map/dot_general | solution.py:66
  91.4 4.2 %collective-permute-start.1 = (bf16[2,128,256]{2,1,0:T(8,128)(2,1)S(1)}, bf16[2,128,256]{2,1,0:T(8,128)(2,1)S(1)}, u32[]{:S(2)}, u32[]{:S(2)}) collective-permute-start(bf16[2,128,256]{2,1,0:T(8,128)(2,1)S(1)} %pad_maximum_fusion.1), channel_id=1, source_target_pairs={{0,30},{2,0},{4,2},{6,4},{8,6},{10,8},{12,10},{14,12},{16,14},{18,... | collective-permute-start | bytes 393224 | tf_op jit(solution)/shard_map/ppermute | solution.py:14
  95.6 0.2 reduce-scatter.9.cloned.1.call-done
  95.8 1.7 %fusion.36 = bf16[1,128,256]{2,1,0:T(8,128)(2,1)S(1)} fusion(bf16[128,1400]{0,1:T(8,128)(2,1)S(1)} %copy-done.1, bf16[256,512]{1,0:T(8,128)(2,1)S(1)} %bitcast.205, bf16[512,1400]{0,1:T(8,128)(2,1)S(1)} %copy-done, bf16[128,256]{1,0:T(8,128)(2,1)} %reduce-scatter.9.cloned.1.call-done), kind=kOutput, calls=%fused_computation.58 | convolution fusion | flops 459241472 | bytes 2185216 | tf_op jit(solution)/shard_map/dot_general | solution.py:66
  97.6 9.0 %reduce-scatter.11.cloned.1.call-done = bf16[128,256]{1,0:T(8,128)(2,1)} async-done(((bf16[256,256]{1,0:T(8,128)(2,1)}), bf16[128,256]{1,0:T(8,128)(2,1)}) %reduce-scatter.11.cloned.1.call-update) | async-done | bytes 65552 | tf_op jit(solution)/shard_map/reduce_scatter | solution.py:60
  106.6 1.7 %fusion.37 = bf16[1,128,256]{2,1,0:T(8,128)(2,1)S(1)} fusion(bf16[128,1400]{0,1:T(8,128)(2,1)S(1)} %copy-done.2, bf16[256,512]{1,0:T(8,128)(2,1)S(1)} %bitcast.204, bf16[512,1400]{0,1:T(8,128)(2,1)S(1)} %copy-done, bf16[128,256]{1,0:T(8,128)(2,1)} %reduce-scatter.11.cloned.1.call-done), kind=kOutput, calls=%fused_computation.59 | convolution fusion | flops 459241472 | bytes 2185216 | tf_op jit(solution)/shard_map/dot_general | solution.py:66
  108.4 4.5 %collective-permute-start.3 = (bf16[2,128,256]{2,1,0:T(8,128)(2,1)S(1)}, bf16[2,128,256]{2,1,0:T(8,128)(2,1)S(1)}, u32[]{:S(2)}, u32[]{:S(2)}) collective-permute-start(bf16[2,128,256]{2,1,0:T(8,128)(2,1)S(1)} %pad_maximum_fusion.2), channel_id=1, source_target_pairs={{0,28},{2,30},{4,0},{6,2},{8,4},{10,6},{12,8},{14,10},{16,12},{18,... | collective-permute-start | bytes 393224 | tf_op jit(solution)/shard_map/ppermute | solution.py:14
  112.9 3.2 %collective-permute-done.3 = bf16[2,128,256]{2,1,0:T(8,128)(2,1)S(1)} collective-permute-done((bf16[2,128,256]{2,1,0:T(8,128)(2,1)S(1)}, bf16[2,128,256]{2,1,0:T(8,128)(2,1)S(1)}, u32[]{:S(2)}, u32[]{:S(2)}) %collective-permute-start.3) | collective-permute-done | bytes 131104 | tf_op jit(solution)/shard_map/ppermute | solution.py:14
  116.2 0.7 copy.27
  (35 shorter events, 0.2 us)
Async XLA Ops:
  6.5 14.4 %copy-start = (bf16[512,1400]{0,1:T(8,128)(2,1)S(1)}, bf16[512,1400]{0,1:T(8,128)(2,1)}, u32[]{:S(2)}) copy-start(bf16[512,1400]{0,1:T(8,128)(2,1)} %param.6) | copy-start | bytes 4300804
  6.5 81.0 %reduce-scatter.5.cloned.1.call-start = ((), (), s32[]{:S(2)}) async-start(), calls=%async_computation.4 | async-start | bytes 196608 | tf_op jit(solution)/shard_map/reduce_scatter | solution.py:60
  6.5 43.5 %collective-permute-start = (bf16[2,32,512]{2,1,0:T(8,128)(2,1)}, bf16[2,32,512]{2,1,0:T(8,128)(2,1)S(1)}, u32[]{:S(2)}, u32[]{:S(2)}) collective-permute-start(bf16[2,32,512]{2,1,0:T(8,128)(2,1)} %param.5), channel_id=1, source_target_pairs={{0,2},{2,4},{4,6},{6,8},{8,10},{10,12},{12,14},{14,16},{16,18},{18... | collective-permute-start | bytes 196616 | tf_op jit(solution)/shard_map/ppermute | solution.py:14
  9.5 40.6 %collective-permute-start.2 = (bf16[2,32,512]{2,1,0:T(8,128)(2,1)}, bf16[2,32,512]{2,1,0:T(8,128)(2,1)S(1)}, u32[]{:S(2)}, u32[]{:S(2)}) collective-permute-start(bf16[2,32,512]{2,1,0:T(8,128)(2,1)} %param.5), channel_id=1, source_target_pairs={{0,4},{2,6},{4,8},{6,10},{8,12},{10,14},{12,16},{14,18},{16,20},{1... | collective-permute-start | bytes 196616 | tf_op jit(solution)/shard_map/ppermute | solution.py:14
  22.9 25.8 %copy-start.9 = (f32[1400]{0:T(1024)S(1)}, f32[1400]{0:T(1024)}, u32[]{:S(2)}) copy-start(f32[1400]{0:T(1024)} %param.8) | copy-start | bytes 16804
  56.6 6.1 %copy-start.8 = (bf16[16,16,512]{2,1,0:T(8,128)(2,1)S(1)}, bf16[16,16,512]{2,1,0:T(8,128)(2,1)}, u32[]{:S(2)}) copy-start(bf16[16,16,512]{2,1,0:T(8,128)(2,1)} %get-tuple-element.29) | copy-start | bytes 786436
  62.5 27.0 %reduce-scatter.7.cloned.1.call-start = ((), (), s32[]{:S(2)}) async-start(), calls=%async_computation.5 | async-start | bytes 196608 | tf_op jit(solution)/shard_map/reduce_scatter | solution.py:60
  75.4 1.6 %copy-start.7 = (bf16[16,16,512]{2,1,0:T(8,128)(2,1)S(1)}, bf16[16,16,512]{2,1,0:T(8,128)(2,1)}, u32[]{:S(2)}) copy-start(bf16[16,16,512]{2,1,0:T(8,128)(2,1)} %get-tuple-element.34) | copy-start | bytes 786436
  77.0 18.8 %reduce-scatter.9.cloned.1.call-start = ((), (), s32[]{:S(2)}) async-start(), calls=%async_computation.6 | async-start | bytes 196608 | tf_op jit(solution)/shard_map/reduce_scatter | solution.py:60
  84.7 21.8 %reduce-scatter.11.cloned.1.call-start = ((), (), s32[]{:S(2)}) async-start(), calls=%async_computation.7 | async-start | bytes 196608 | tf_op jit(solution)/shard_map/reduce_scatter | solution.py:60
  84.8 2.7 %copy-start.6 = (bf16[16,16,512]{2,1,0:T(8,128)(2,1)S(1)}, bf16[16,16,512]{2,1,0:T(8,128)(2,1)}, u32[]{:S(2)}) copy-start(bf16[16,16,512]{2,1,0:T(8,128)(2,1)} %get-tuple-element.43) | copy-start | bytes 786436
  87.5 2.0 %copy-start.2 = (bf16[128,1400]{0,1:T(8,128)(2,1)S(1)}, bf16[128,1400]{0,1:T(8,128)(2,1)}, u32[]{:S(2)}) copy-start(bf16[128,1400]{0,1:T(8,128)(2,1)} %fusion.2) | copy-start | bytes 1075204
  87.5 2.1 %copy-start.5 = (bf16[16,16,512]{2,1,0:T(8,128)(2,1)S(1)}, bf16[16,16,512]{2,1,0:T(8,128)(2,1)}, u32[]{:S(2)}) copy-start(bf16[16,16,512]{2,1,0:T(8,128)(2,1)} %get-tuple-element.30) | copy-start | bytes 786436
  89.5 6.3 %copy-start.1 = (bf16[128,1400]{0,1:T(8,128)(2,1)S(1)}, bf16[128,1400]{0,1:T(8,128)(2,1)}, u32[]{:S(2)}) copy-start(bf16[128,1400]{0,1:T(8,128)(2,1)} %fusion.5) | copy-start | bytes 1075204
  89.5 6.3 %copy-start.4 = (bf16[16,16,512]{2,1,0:T(8,128)(2,1)S(1)}, bf16[16,16,512]{2,1,0:T(8,128)(2,1)}, u32[]{:S(2)}) copy-start(bf16[16,16,512]{2,1,0:T(8,128)(2,1)} %get-tuple-element.40) | copy-start | bytes 786436
  91.4 15.2 %copy-start.3 = (bf16[16,16,512]{2,1,0:T(8,128)(2,1)S(1)}, bf16[16,16,512]{2,1,0:T(8,128)(2,1)}, u32[]{:S(2)}) copy-start(bf16[16,16,512]{2,1,0:T(8,128)(2,1)} %get-tuple-element.33) | copy-start | bytes 786436
  91.4 21.5 %collective-permute-start.1 = (bf16[2,128,256]{2,1,0:T(8,128)(2,1)S(1)}, bf16[2,128,256]{2,1,0:T(8,128)(2,1)S(1)}, u32[]{:S(2)}, u32[]{:S(2)}) collective-permute-start(bf16[2,128,256]{2,1,0:T(8,128)(2,1)S(1)} %pad_maximum_fusion.1), channel_id=1, source_target_pairs={{0,30},{2,0},{4,2},{6,4},{8,6},{10,8},{12,10},{14,12},{16,14},{18,... | collective-permute-start | bytes 393224 | tf_op jit(solution)/shard_map/ppermute | solution.py:14
  108.4 7.8 %collective-permute-start.3 = (bf16[2,128,256]{2,1,0:T(8,128)(2,1)S(1)}, bf16[2,128,256]{2,1,0:T(8,128)(2,1)S(1)}, u32[]{:S(2)}, u32[]{:S(2)}) collective-permute-start(bf16[2,128,256]{2,1,0:T(8,128)(2,1)S(1)} %pad_maximum_fusion.2), channel_id=1, source_target_pairs={{0,28},{2,30},{4,0},{6,2},{8,4},{10,6},{12,8},{14,10},{16,12},{18,... | collective-permute-start | bytes 393224 | tf_op jit(solution)/shard_map/ppermute | solution.py:14
Sparse Core Ops, SparseCore 0:
  62.6 7.7 reduce-scatter.4
  77.1 7.7 reduce-scatter.6
  87.1 8.6 reduce-scatter.8
  97.9 8.6 reduce-scatter.10
where the time goes:
time: 124 us; the launch traced here: 123 us
  local copies, waits for them, and re-layouts  40.3 us (32%)
  matrix products  33.4 us (27%)
  between operations  21 us (17%)
  starting transfers between devices  13.5 us (11%)
  waiting for transfers between devices  12.6 us (10%)
  other arithmetic  2.66 us (2%)
    dynamic_slice x1, local copies, waits for them, and re-layouts, shards(): interaction = lax.dynamic_index_in_dim(screen, q_pick, 0, keepdims=False)  25.8 us
    ppermute x4, starting transfers between devices, from_behind(): return lax.ppermute(value, axis, pairs)  13.2 us
    dot_general x4, matrix products, shards(): screened = jnp.dot(cond, interaction, preferred_element_type=jnp.float32)  13.1 us
    reduce_scatter x4, waiting for transfers between devices, shards(): lax.psum_scatter(terms.reshape(val_rows * NC * lax.axis_size('pair'), NV...  9.28 us
    dot_general x4, matrix products, shards(): jnp.einsum('xyg,vwg->vxwy', screened, vale, preferred_element_type=jnp.fl...  8.13 us
    convert_element_type x4, local copies, waits for them, and re-layouts, shards(): terms.reshape(val_rows * NC * lax.axis_size('pair'), NV * NC)  7.79 us
    dot_general x4, matrix products, shards(): lax.dot_general(own_weighted[local_k], pair_fields(column_orbital[:NV], c...  7.24 us
    dot_general x6, matrix products, pair_fields(): jnp.dot(flat, fitting, preferred_element_type=jnp.float32)  4.86 us
  transfers between devices with their start and end apart: 8, of which 3 were waited for; matrix products, arithmetic and copies ran while one was open for 51% of the time, Pallas kernels for 0%

commit v1 on v0

v1 whole, which is shorter than its diff:
```python
import functools
import jax
import jax.numpy as jnp
from jax import lax
from jax.experimental import pallas as pl
from jax.experimental.pallas import tpu as pltpu
from jax.sharding import PartitionSpec as P

NV = 16
NC = 16
S = 2
LANES = 128
MESH = pl.DeviceIdType.MESH
NT = (((1,), (1,)), ((), ()))


def dot(left, right):
    return jnp.dot(left, right, preferred_element_type=jnp.float32)


def dot_nt(left, right):
    return lax.dot_general(left, right, NT, preferred_element_type=jnp.float32)


def products(major, minor):
    both = major[:, None, :] * minor[None, :, :]
    return both.astype(jnp.bfloat16).reshape(major.shape[0] * minor.shape[0], major.shape[1])


def chunks_of(width, n_q):
    for count in (5, 7, 4, 3, 2):
        if width % count == 0 and width // count * n_q % 16 == 0:
            return count
    return 1


def exchange_digits(value):
    lane = lax.broadcasted_iota(jnp.int32, (16, LANES), 1)
    halves = []
    for half in range(value.shape[1] // LANES):
        groups = [
            value[16 * g : 16 * g + 16, half * LANES : (half + 1) * LANES] for g in range(16)
        ]
        for bit in range(4):
            step = 1 << bit
            odd = (lane // step) % 2 == 1
            later = list(groups)
            for g in range(16):
                if g & step == 0:
                    low, high = groups[g], groups[g + step]
                    later[g] = jnp.where(odd, pltpu.roll(high, step, 1), low)
                    later[g + step] = jnp.where(odd, high, pltpu.roll(low, LANES - step, 1))
            groups = later
        halves.append(jnp.concatenate(groups, axis=0))
    return jnp.concatenate(halves, axis=1)


def body(
    loop_count,
    pair_count,
    orb_ref,
    coul_ref,
    q_ref,
    fit_hbm,
    screen_hbm,
    out_ref,
    fit,
    screen,
    fit_own,
    mixed,
    between,
    turned,
    arrived,
    part,
    leaving,
    landed,
    fit_sem,
    screen_sem,
    orb_send,
    orb_recv,
    part_send,
    part_recv,
):
    per_dev = orb_ref.shape[0]
    width, n_q, n_g = screen.shape
    rows = NV * NC // pair_count
    me = lax.axis_index("kloop")
    side = lax.axis_index("pair")
    chunks = chunks_of(width, n_q)
    chunk = width // chunks

    def fetch(index):
        span = pl.ds(index * chunk, chunk)
        return pltpu.make_async_copy(screen_hbm.at[span], screen.at[span], screen_sem.at[index])

    fit_copy = pltpu.make_async_copy(fit_hbm, fit, fit_sem)
    fit_copy.start()
    for index in range(chunks):
        fetch(index).start()

    barrier = pltpu.get_barrier_semaphore()
    for shift in range(1, S + 1):
        source = lax.rem(me + shift, loop_count)
        pl.semaphore_signal(barrier, inc=1, device_id={"kloop": source}, device_id_type=MESH)
    for offset in range(1, pair_count):
        other = lax.rem(side + offset, pair_count)
        pl.semaphore_signal(barrier, inc=1, device_id={"pair": other}, device_id_type=MESH)

    fit_copy.wait()
    for index in range(pair_count):

        @pl.when(side == index)
        def _():
            own = fit[index * width : (index + 1) * width, :]
            across = own.T
            fit_own[...] = across
            weight = coul_ref[:, index * width : (index + 1) * width]
            weighted = (across.astype(jnp.float32) * weight).astype(jnp.bfloat16)
            coupling = dot(weighted, own).astype(jnp.bfloat16)
            for k in range(per_dev):
                orb = orb_ref[k].astype(jnp.float32)
                turned[k] = dot(products(orb[:NV], orb[NV:]), coupling).astype(jnp.bfloat16)

    pl.semaphore_wait(barrier, S + pair_count - 1)
    orb_copies = []
    for shift in range(1, S + 1):
        target = lax.rem(me - shift + loop_count, loop_count)
        orb_copies.append(
            pltpu.make_async_remote_copy(
                src_ref=orb_ref,
                dst_ref=arrived.at[shift - 1],
                send_sem=orb_send.at[shift - 1],
                recv_sem=orb_recv.at[shift - 1],
                device_id={"kloop": target},
                device_id_type=MESH,
            )
        )
        orb_copies[-1].start()

    @pl.loop(0, chunks)
    def _(index):
        fetch(index).wait()
        taken = screen[pl.ds(index * chunk, chunk)].reshape(chunk * n_q, n_g)
        start = pl.multiple_of(index * chunk * n_q, 8)
        result = dot(taken, fit[...])
        for tile in range(result.shape[1] // LANES):
            mixed[tile, pl.ds(start, chunk * n_q), :] = result[:, tile * LANES : (tile + 1) * LANES]

    for q in range(n_q):
        half = jnp.concatenate(
            [mixed[tile, pl.ds(q, width, stride=n_q), :] for tile in range(mixed.shape[0])], axis=1
        )
        between[q] = dot(fit_own[...], half.astype(jnp.bfloat16)).astype(jnp.bfloat16)

    part_copies = []
    for shift in range(1, S + 1):
        orb_copies[shift - 1].wait()
        for k in range(per_dev):
            block = (shift - 1) * per_dev + k
            row = arrived[shift - 1, k].astype(jnp.float32)
            col = orb_ref[k].astype(jnp.float32)
            q = q_ref[shift - 1, me * per_dev + k]
            cond = products(col[NV:], row[NV:])
            screened = dot_nt(cond, between[q]).astype(jnp.bfloat16)
            direct = exchange_digits(dot_nt(screened, products(col[:NV], row[:NV])))
            exchange = dot_nt(products(row[:NV], row[NV:]), turned[k])
            total = 2.0 * exchange - direct
            part[block] = total
            leaving[block] = total.astype(jnp.bfloat16)
            for offset in range(1, pair_count):
                other = lax.rem(side + offset, pair_count)
                copy = pltpu.make_async_remote_copy(
                    src_ref=leaving.at[block, pl.ds(pl.multiple_of(other * rows, rows), rows)],
                    dst_ref=landed.at[block, offset - 1],
                    send_sem=part_send.at[block, offset - 1],
                    recv_sem=part_recv.at[block, offset - 1],
                    device_id={"pair": other},
                    device_id_type=MESH,
                )
                copy.start()
                part_copies.append(copy)

    for shift in range(1, S + 1):
        for k in range(per_dev):
            block = (shift - 1) * per_dev + k
            total = part[block, pl.ds(pl.multiple_of(side * rows, rows), rows), :]
            for offset in range(1, pair_count):
                part_copies[block * (pair_count - 1) + offset - 1].wait()
                total = total + landed[block, offset - 1].astype(jnp.float32)
            out_ref[k, shift - 1] = total.astype(jnp.bfloat16)


def shards(orbitals, fitting, screen, coulomb, qindex):
    per_dev, bands, points = orbitals.shape
    pair_count = lax.axis_size("pair")
    loop_count = lax.axis_size("kloop")
    n_q, n_g, width = screen.shape
    rows = NV * NC // pair_count
    blocks = S * per_dev
    n = NV * NC
    flops = 2 * n_q * points * width * (n_g + points) + 2 * points * points * width
    flops += blocks * 2 * n * points * (points + 2 * n)
    vmem = pl.BlockSpec(memory_space=pltpu.VMEM)
    dma = pltpu.SemaphoreType.DMA
    return pl.pallas_call(
        functools.partial(body, loop_count, pair_count),
        out_shape=jax.ShapeDtypeStruct((per_dev, S, rows, n), jnp.bfloat16),
        in_specs=[
            vmem,
            vmem,
            pl.BlockSpec(memory_space=pltpu.SMEM),
            pl.BlockSpec(memory_space=pl.ANY),
            pl.BlockSpec(memory_space=pl.ANY),
        ],
        out_specs=vmem,
        scratch_shapes=[
            pltpu.VMEM((n_g, points), jnp.bfloat16),
            pltpu.VMEM((width, n_q, n_g), jnp.bfloat16),
            pltpu.VMEM((points, width), jnp.bfloat16),
            pltpu.VMEM((points // LANES, width * n_q, LANES), jnp.float32),
            pltpu.VMEM((n_q, points, points), jnp.bfloat16),
            pltpu.VMEM((per_dev, n, points), jnp.bfloat16),
            pltpu.VMEM((S, per_dev, bands, points), jnp.bfloat16),
            pltpu.VMEM((blocks, n, n), jnp.float32),
            pltpu.VMEM((blocks, n, n), jnp.bfloat16),
            pltpu.VMEM((blocks, max(pair_count - 1, 1), rows, n), jnp.bfloat16),
            dma,
            dma((chunks_of(width, n_q),)),
            dma((S,)),
            dma((S,)),
            dma((blocks, max(pair_count - 1, 1))),
            dma((blocks, max(pair_count - 1, 1))),
        ],
        compiler_params=pltpu.CompilerParams(
            collective_id=0, has_side_effects=True, vmem_limit_bytes=52 * 1024 * 1024
        ),
        cost_estimate=pl.CostEstimate(
            flops=flops, bytes_accessed=2 * (n_q * n_g * width + points * n_g), transcendentals=0
        ),
    )(orbitals, coulomb.reshape(1, n_g), qindex.T, fitting.T, jnp.transpose(screen, (2, 0, 1)))


def solution(mesh):
    return jax.shard_map(
        shards,
        mesh=mesh,
        in_specs=(P("kloop", None, None), P(), P(None, None, "pair"), P(), P()),
        out_specs=P("kloop", None, "pair", None),
        check_vma=False,
    )
```

time: 124 us -> 23.8 us (0.19)
  local copies, waits for them, and re-layouts: 40.3 us -> 4.28 us
  matrix products: 33.4 us -> 0 us
  between operations: 21 us -> 0.01 us
  Pallas kernels: 0 us -> 19.2 us
  starting transfers between devices: 13.5 us -> 0 us
  waiting for transfers between devices: 12.6 us -> 0 us
  other arithmetic: 2.66 us -> 0 us
    dot_general x18 -> x0, matrix products: 33.4 us -> none  [the longest x4 13.1 us: shards(): screened = jnp.dot(cond, interaction, preferred_element_type=jnp.float32)]
    dynamic_slice x2 -> x0, local copies, waits for them, and re-layouts: 27.3 us -> none  [the longest x1 25.8 us: shards(): interaction = lax.dynamic_index_in_dim(screen, q_pick, 0, keepdims=False)]
    pallas_call x0 -> x1, Pallas kernels: none -> 19.2 us  [shards(): pl.pallas_call(functools.partial(body, loop_count, pair_count), out_shape...]
    ppermute x4 -> x0, starting transfers between devices: 13.2 us -> none  [from_behind(): return lax.ppermute(value, axis, pairs)]
    convert_element_type x12 -> x0, local copies, waits for them, and re-layouts: 12.3 us -> none  [the longest x4 7.79 us: shards(): terms.reshape(val_rows * NC * lax.axis_size('pair'), NV * NC)]
    reduce_scatter x4 -> x0, waiting for transfers between devices: 9.28 us -> none  [shards(): lax.psum_scatter(terms.reshape(val_rows * NC * lax.axis_size('pair'), NV...]
    unnamed x20 -> x7, local copies, waits for them, and re-layouts: 0.04 us -> 3.58 us
    ppermute x4 -> x0, waiting for transfers between devices: 3.24 us -> none  [from_behind(): return lax.ppermute(value, axis, pairs)]
  transfers between devices with their start and end apart: 8 -> 0, of which waited for: 3 -> 0; matrix products, arithmetic and copies ran while one was open for 51% -> 0% of each run, Pallas kernels for 0% -> 0%
where the time goes in v1:
time: 23.8 us; the launch traced here: 23.5 us
  Pallas kernels  19.2 us (81%)
  local copies, waits for them, and re-layouts  4.28 us (18%)
    pallas_call x1, Pallas kernels, shards(): pl.pallas_call(functools.partial(body, loop_count, pair_count), out_shape...  19.2 us
    unnamed x7, local copies, waits for them, and re-layouts  3.58 us
    reshape x1, local copies, waits for them, and re-layouts, shards(): coulomb.reshape(1, n_g)  0.7 us

profile of v1, /device:TPU:0, one launch (start us, length us, event | category | flops | bytes accessed | tf_op | source)
XLA Modules:
  0.0 23.5 jit_solution(6848576532927932363)
XLA Ops:
  0.0 0.7 %reshape.3.coul_ref = f32[1,1400]{1,0:T(1,128)S(1)} reshape(f32[1400]{0:T(1024)} %param.8) | data formatting | bytes 11200 | tf_op jit(solution)/shard_map/reshape | solution.py:240
  0.7 0.0 copy-start
  0.7 1.4 %copy-done = bf16[512,1400]{0,1:T(8,128)(2,1)S(1)} copy-done((bf16[512,1400]{0,1:T(8,128)(2,1)S(1)}, bf16[512,1400]{0,1:T(8,128)(2,1)}, u32[]{:S(2)}) %copy-start) | copy-done | bytes 1433624
  2.1 0.0 copy-start.1
  2.1 0.8 %copy-done.1 = bf16[2,32,512]{2,1,0:T(8,128)(2,1)S(1)} copy-done((bf16[2,32,512]{2,1,0:T(8,128)(2,1)S(1)}, bf16[2,32,512]{2,1,0:T(8,128)(2,1)}, u32[]{:S(2)}) %copy-start.1) | copy-done | bytes 65560
  2.9 0.0 copy-start.2
  2.9 0.7 %copy-done.2 = s32[32,2]{0,1:T(2,128)S(1)} copy-done((s32[32,2]{0,1:T(2,128)S(1)}, s32[32,2]{0,1:T(2,128)}, u32[]{:S(2)}) %copy-start.2) | copy-done | bytes 280
  3.6 19.2 %shard_map.55 = bf16[2,2,128,256]{3,2,1,0:T(8,128)(2,1)S(1)} custom-call(bf16[2,32,512]{2,1,0:T(8,128)(2,1)S(1)} %copy-done.1, f32[1,1400]{1,0:T(1,128)S(1)} %reshape.3.coul_ref, s32[2,32]{1,0:T(2,128)S(1)} %bitcast.4, bf16[1400,512]{1,0:T(8,128)(2,1)S(1)} %bitcast.3, bf16[700,4,1400]{2,1,0:T(4,128)(2,1)} %bitcast.5), custom_call_target="tpu_custom_call" | custom-call | flops 6922829824 | bytes 9273600 | tf_op jit(solution)/shard_map/pallas_call | solution.py:205
  22.8 0.7 %copy.7 = bf16[2,2,128,256]{3,2,1,0:T(8,128)(2,1)} copy(bf16[2,2,128,256]{3,2,1,0:T(8,128)(2,1)S(1)} %shard_map.55) | data formatting | bytes 524288
Async XLA Ops:
  0.7 1.4 %copy-start = (bf16[512,1400]{0,1:T(8,128)(2,1)S(1)}, bf16[512,1400]{0,1:T(8,128)(2,1)}, u32[]{:S(2)}) copy-start(bf16[512,1400]{0,1:T(8,128)(2,1)} %param.6) | copy-start | bytes 4300804
  2.1 0.8 %copy-start.1 = (bf16[2,32,512]{2,1,0:T(8,128)(2,1)S(1)}, bf16[2,32,512]{2,1,0:T(8,128)(2,1)}, u32[]{:S(2)}) copy-start(bf16[2,32,512]{2,1,0:T(8,128)(2,1)} %orb_ref.1) | copy-start | bytes 196612
  2.9 0.7 %copy-start.2 = (s32[32,2]{0,1:T(2,128)S(1)}, s32[32,2]{0,1:T(2,128)}, u32[]{:S(2)}) copy-start(s32[32,2]{0,1:T(2,128)} %param.9) | copy-start | bytes 772

commit v2 on v1

--- a/solution.py
+++ b/solution.py
@@ -58,12 +58,15 @@
 def body(
     loop_count,
     pair_count,
+    orb_hbm,
+    coul_hbm,
+    q_hbm,
+    fit_hbm,
+    screen_hbm,
+    out_ref,
     orb_ref,
     coul_ref,
     q_ref,
-    fit_hbm,
-    screen_hbm,
-    out_ref,
     fit,
     screen,
     fit_own,
@@ -74,6 +77,9 @@
     part,
     leaving,
     landed,
+    orb_sem,
+    coul_sem,
+    q_sem,
     fit_sem,
     screen_sem,
     orb_send,
@@ -94,7 +100,11 @@
         return pltpu.make_async_copy(screen_hbm.at[span], screen.at[span], screen_sem.at[index])
 
     fit_copy = pltpu.make_async_copy(fit_hbm, fit, fit_sem)
-    fit_copy.start()
+    orb_copy = pltpu.make_async_copy(orb_hbm, orb_ref, orb_sem)
+    coul_copy = pltpu.make_async_copy(coul_hbm, coul_ref, coul_sem)
+    q_copy = pltpu.make_async_copy(q_hbm, q_ref, q_sem)
+    for copy in (orb_copy, coul_copy, q_copy, fit_copy):
+        copy.start()
     for index in range(chunks):
         fetch(index).start()
 
@@ -106,7 +116,9 @@
         other = lax.rem(side + offset, pair_count)
         pl.semaphore_signal(barrier, inc=1, device_id={"pair": other}, device_id_type=MESH)
 
-    fit_copy.wait()
+    for copy in (orb_copy, coul_copy, q_copy, fit_copy):
+        copy.wait()
+    all_weights = coul_ref[...].reshape(1, n_g)
     for index in range(pair_count):
 
         @pl.when(side == index)
@@ -114,7 +126,7 @@
             own = fit[index * width : (index + 1) * width, :]
             across = own.T
             fit_own[...] = across
-            weight = coul_ref[:, index * width : (index + 1) * width]
+            weight = all_weights[:, index * width : (index + 1) * width]
             weighted = (across.astype(jnp.float32) * weight).astype(jnp.bfloat16)
             coupling = dot(weighted, own).astype(jnp.bfloat16)
             for k in range(per_dev):
@@ -206,14 +218,17 @@
         functools.partial(body, loop_count, pair_count),
         out_shape=jax.ShapeDtypeStruct((per_dev, S, rows, n), jnp.bfloat16),
         in_specs=[
-            vmem,
-            vmem,
-            pl.BlockSpec(memory_space=pltpu.SMEM),
-            pl.BlockSpec(memory_space=pl.ANY),
-            pl.BlockSpec(memory_space=pl.ANY),
+            pl.BlockSpec(memory_space=pltpu.HBM),
+            pl.BlockSpec(memory_space=pltpu.HBM),
+            pl.BlockSpec(memory_space=pltpu.HBM),
+            pl.BlockSpec(memory_space=pltpu.HBM),
+            pl.BlockSpec(memory_space=pltpu.HBM),
         ],
         out_specs=vmem,
         scratch_shapes=[
+            pltpu.VMEM((per_dev, bands, points), jnp.bfloat16),
+            pltpu.VMEM((n_g,), jnp.float32),
+            pltpu.SMEM((S, per_dev * loop_count), jnp.int32),
             pltpu.VMEM((n_g, points), jnp.bfloat16),
             pltpu.VMEM((width, n_q, n_g), jnp.bfloat16),
             pltpu.VMEM((points, width), jnp.bfloat16),
@@ -225,6 +240,9 @@
             pltpu.VMEM((blocks, n, n), jnp.bfloat16),
             pltpu.VMEM((blocks, max(pair_count - 1, 1), rows, n), jnp.bfloat16),
             dma,
+            dma,
+            dma,
+            dma,
             dma((chunks_of(width, n_q),)),
             dma((S,)),
             dma((S,)),
@@ -232,12 +250,12 @@
             dma((blocks, max(pair_count - 1, 1))),
         ],
         compiler_params=pltpu.CompilerParams(
-            collective_id=0, has_side_effects=True, vmem_limit_bytes=52 * 1024 * 1024
+            collective_id=0, has_side_effects=True, vmem_limit_bytes=64 * 1024 * 1024
         ),
         cost_estimate=pl.CostEstimate(
             flops=flops, bytes_accessed=2 * (n_q * n_g * width + points * n_g), transcendentals=0
         ),
-    )(orbitals, coulomb.reshape(1, n_g), qindex.T, fitting.T, jnp.transpose(screen, (2, 0, 1)))
+    )(orbitals, coulomb, qindex.T, fitting.T, jnp.transpose(screen, (2, 0, 1)))
 
 
 def solution(mesh):

time: 23.8 us -> 21 us (0.88)
  local copies, waits for them, and re-layouts: 4.28 us -> 1.67 us
    unnamed x7 -> x1, local copies, waits for them, and re-layouts: 3.58 us -> 1.67 us
    reshape x1 -> x0, local copies, waits for them, and re-layouts: 0.7 us -> none  [shards(): coulomb.reshape(1, n_g)]
where the time goes in v2:
time: 21 us; the launch traced here: 20.8 us
  Pallas kernels  19.2 us (91%)
  local copies, waits for them, and re-layouts  1.67 us (8%)
    pallas_call x1, Pallas kernels, shards(): pl.pallas_call(functools.partial(body, loop_count, pair_count), out_shape...  19.2 us
    unnamed x1, local copies, waits for them, and re-layouts  1.67 us

profile of v2, /device:TPU:0, one launch (start us, length us, event | category | flops | bytes accessed | tf_op | source)
XLA Modules:
  0.0 20.8 jit_solution(10345616860368132872)
XLA Ops:
  0.0 19.2 %shard_map.55 = bf16[2,2,128,256]{3,2,1,0:T(8,128)(2,1)} custom-call(bf16[2,32,512]{2,1,0:T(8,128)(2,1)} %orb_hbm.1, f32[1400]{0:T(1024)} %coul_hbm.1, s32[2,32]{1,0:T(2,128)} %bitcast.5, bf16[1400,512]{1,0:T(8,128)(2,1)} %bitcast.4, bf16[700,4,1400]{2,1,0:T(4,128)(2,1)} %bitcast.3), custom_call_target="tpu_custom_call" | custom-call | flops 6922829824 | bytes 9273600 | tf_op jit(solution)/shard_map/pallas_call | solution.py:217
  19.2 1.7 %copy.7 = bf16[2,2,128,256]{3,2,1,0:T(8,128)(2,1)} copy(bf16[2,2,128,256]{3,2,1,0:T(8,128)(2,1)} %shard_map.55) | data formatting | bytes 524288

commit v3 on v2

--- a/solution.py
+++ b/solution.py
@@ -105,9 +105,6 @@
     q_copy = pltpu.make_async_copy(q_hbm, q_ref, q_sem)
     for copy in (orb_copy, coul_copy, q_copy, fit_copy):
         copy.start()
-    for index in range(chunks):
-        fetch(index).start()
-
     barrier = pltpu.get_barrier_semaphore()
     for shift in range(1, S + 1):
         source = lax.rem(me + shift, loop_count)
@@ -116,8 +113,26 @@
         other = lax.rem(side + offset, pair_count)
         pl.semaphore_signal(barrier, inc=1, device_id={"pair": other}, device_id_type=MESH)
 
-    for copy in (orb_copy, coul_copy, q_copy, fit_copy):
+    pl.semaphore_wait(barrier, S + pair_count - 1)
+    orb_copies = []
+    for shift in range(1, S + 1):
+        target = lax.rem(me - shift + loop_count, loop_count)
+        orb_copies.append(
+            pltpu.make_async_remote_copy(
+                src_ref=orb_hbm,
+                dst_ref=arrived.at[shift - 1],
+                send_sem=orb_send.at[shift - 1],
+                recv_sem=orb_recv.at[shift - 1],
+                device_id={"kloop": target},
+                device_id_type=MESH,
+            )
+        )
+        orb_copies[-1].start()
+
+    for copy in (fit_copy, orb_copy, coul_copy, q_copy):
         copy.wait()
+    for index in range(chunks):
+        fetch(index).start()
     all_weights = coul_ref[...].reshape(1, n_g)
     for index in range(pair_count):
 
@@ -133,24 +148,7 @@
                 orb = orb_ref[k].astype(jnp.float32)
                 turned[k] = dot(products(orb[:NV], orb[NV:]), coupling).astype(jnp.bfloat16)
 
-    pl.semaphore_wait(barrier, S + pair_count - 1)
-    orb_copies = []
-    for shift in range(1, S + 1):
-        target = lax.rem(me - shift + loop_count, loop_count)
-        orb_copies.append(
-            pltpu.make_async_remote_copy(
-                src_ref=orb_ref,
-                dst_ref=arrived.at[shift - 1],
-                send_sem=orb_send.at[shift - 1],
-                recv_sem=orb_recv.at[shift - 1],
-                device_id={"kloop": target},
-                device_id_type=MESH,
-            )
-        )
-        orb_copies[-1].start()
-
-    @pl.loop(0, chunks)
-    def _(index):
+    for index in range(chunks):
         fetch(index).wait()
         taken = screen[pl.ds(index * chunk, chunk)].reshape(chunk * n_q, n_g)
         start = pl.multiple_of(index * chunk * n_q, 8)

time: 21 us -> 22.1 us (1.052)
  Pallas kernels: 19.2 us -> 20.3 us
    pallas_call x1, Pallas kernels: 19.2 us -> 20.3 us  [shards(): pl.pallas_call(functools.partial(body, loop_count, pair_count), out_shape...]
where the time goes in v3:
time: 22.1 us; the launch traced here: 22 us
  Pallas kernels  20.3 us (92%)
  local copies, waits for them, and re-layouts  1.67 us (8%)
    pallas_call x1, Pallas kernels, shards(): pl.pallas_call(functools.partial(body, loop_count, pair_count), out_shape...  20.3 us
    unnamed x1, local copies, waits for them, and re-layouts  1.67 us

profile of v3, /device:TPU:0, one launch (start us, length us, event | category | flops | bytes accessed | tf_op | source)
XLA Modules:
  0.0 22.0 jit_solution(16496830437857174114)
XLA Ops:
  0.0 20.3 %shard_map.55 = bf16[2,2,128,256]{3,2,1,0:T(8,128)(2,1)} custom-call(bf16[2,32,512]{2,1,0:T(8,128)(2,1)} %orb_hbm.1, f32[1400]{0:T(1024)} %coul_hbm.1, s32[2,32]{1,0:T(2,128)} %bitcast.5, bf16[1400,512]{1,0:T(8,128)(2,1)} %bitcast.4, bf16[700,4,1400]{2,1,0:T(4,128)(2,1)} %bitcast.3), custom_call_target="tpu_custom_call" | custom-call | flops 6922829824 | bytes 9273600 | tf_op jit(solution)/shard_map/pallas_call | solution.py:215
  20.3 1.7 %copy.7 = bf16[2,2,128,256]{3,2,1,0:T(8,128)(2,1)} copy(bf16[2,2,128,256]{3,2,1,0:T(8,128)(2,1)} %shard_map.55) | data formatting | bytes 524288

commit v4 on v2

--- a/solution.py
+++ b/solution.py
@@ -149,8 +149,7 @@
         )
         orb_copies[-1].start()
 
-    @pl.loop(0, chunks)
-    def _(index):
+    for index in range(chunks):
         fetch(index).wait()
         taken = screen[pl.ds(index * chunk, chunk)].reshape(chunk * n_q, n_g)
         start = pl.multiple_of(index * chunk * n_q, 8)

time: 21 us -> 20.7 us (0.986)
  Pallas kernels: 19.2 us -> 18.9 us
    pallas_call x1, Pallas kernels: 19.2 us -> 18.9 us  [shards(): pl.pallas_call(functools.partial(body, loop_count, pair_count), out_shape...]
where the time goes in v4:
time: 20.7 us; the launch traced here: 20.6 us
  Pallas kernels  18.9 us (91%)
  local copies, waits for them, and re-layouts  1.67 us (8%)
    pallas_call x1, Pallas kernels, shards(): pl.pallas_call(functools.partial(body, loop_count, pair_count), out_shape...  18.9 us
    unnamed x1, local copies, waits for them, and re-layouts  1.67 us

profile of v4, /device:TPU:0, one launch (start us, length us, event | category | flops | bytes accessed | tf_op | source)
XLA Modules:
  0.0 20.6 jit_solution(8927728855353251350)
XLA Ops:
  0.0 18.9 %shard_map.55 = bf16[2,2,128,256]{3,2,1,0:T(8,128)(2,1)} custom-call(bf16[2,32,512]{2,1,0:T(8,128)(2,1)} %orb_hbm.1, f32[1400]{0:T(1024)} %coul_hbm.1, s32[2,32]{1,0:T(2,128)} %bitcast.5, bf16[1400,512]{1,0:T(8,128)(2,1)} %bitcast.4, bf16[700,4,1400]{2,1,0:T(4,128)(2,1)} %bitcast.3), custom_call_target="tpu_custom_call" | custom-call | flops 6922829824 | bytes 9273600 | tf_op jit(solution)/shard_map/pallas_call | solution.py:216
  18.9 1.7 %copy.7 = bf16[2,2,128,256]{3,2,1,0:T(8,128)(2,1)} copy(bf16[2,2,128,256]{3,2,1,0:T(8,128)(2,1)} %shard_map.55) | data formatting | bytes 524288

commit v5 on v3

--- a/solution.py
+++ b/solution.py
@@ -105,6 +105,9 @@
     q_copy = pltpu.make_async_copy(q_hbm, q_ref, q_sem)
     for copy in (orb_copy, coul_copy, q_copy, fit_copy):
         copy.start()
+    for index in range(chunks):
+        fetch(index).start()
+
     barrier = pltpu.get_barrier_semaphore()
     for shift in range(1, S + 1):
         source = lax.rem(me + shift, loop_count)
@@ -113,13 +116,15 @@
         other = lax.rem(side + offset, pair_count)
         pl.semaphore_signal(barrier, inc=1, device_id={"pair": other}, device_id_type=MESH)
 
+    for copy in (orb_copy, coul_copy, q_copy, fit_copy):
+        copy.wait()
     pl.semaphore_wait(barrier, S + pair_count - 1)
     orb_copies = []
     for shift in range(1, S + 1):
         target = lax.rem(me - shift + loop_count, loop_count)
         orb_copies.append(
             pltpu.make_async_remote_copy(
-                src_ref=orb_hbm,
+                src_ref=orb_ref,
                 dst_ref=arrived.at[shift - 1],
                 send_sem=orb_send.at[shift - 1],
                 recv_sem=orb_recv.at[shift - 1],
@@ -129,10 +134,6 @@
         )
         orb_copies[-1].start()
 
-    for copy in (fit_copy, orb_copy, coul_copy, q_copy):
-        copy.wait()
-    for index in range(chunks):
-        fetch(index).start()
     all_weights = coul_ref[...].reshape(1, n_g)
     for index in range(pair_count):
 

time: 22.1 us -> 21.7 us (0.982)
  Pallas kernels: 20.3 us -> 19.9 us
    pallas_call x1, Pallas kernels: 20.3 us -> 19.9 us  [shards(): pl.pallas_call(functools.partial(body, loop_count, pair_count), out_shape...]
where the time goes in v5:
time: 21.7 us; the launch traced here: 21.6 us
  Pallas kernels  19.9 us (92%)
  local copies, waits for them, and re-layouts  1.67 us (8%)
    pallas_call x1, Pallas kernels, shards(): pl.pallas_call(functools.partial(body, loop_count, pair_count), out_shape...  19.9 us
    unnamed x1, local copies, waits for them, and re-layouts  1.67 us

profile of v5, /device:TPU:0, one launch (start us, length us, event | category | flops | bytes accessed | tf_op | source)
XLA Modules:
  0.0 21.6 jit_solution(11284255233404312129)
XLA Ops:
  0.0 19.9 %shard_map.55 = bf16[2,2,128,256]{3,2,1,0:T(8,128)(2,1)} custom-call(bf16[2,32,512]{2,1,0:T(8,128)(2,1)} %orb_hbm.1, f32[1400]{0:T(1024)} %coul_hbm.1, s32[2,32]{1,0:T(2,128)} %bitcast.5, bf16[1400,512]{1,0:T(8,128)(2,1)} %bitcast.4, bf16[700,4,1400]{2,1,0:T(4,128)(2,1)} %bitcast.3), custom_call_target="tpu_custom_call" | custom-call | flops 6922829824 | bytes 9273600 | tf_op jit(solution)/shard_map/pallas_call | solution.py:216
  19.9 1.7 %copy.7 = bf16[2,2,128,256]{3,2,1,0:T(8,128)(2,1)} copy(bf16[2,2,128,256]{3,2,1,0:T(8,128)(2,1)} %shard_map.55) | data formatting | bytes 524288
